TPU v7x, 1024 devices: a whole 4x8x16 slice. The times are simulated.
1024 devices in a mesh: tens: 64 (over x, z), tile: 16 (over y, core).
Axes of the slice: x: 4, y: 8, z: 16, core: 2. Of those that a mesh axis runs over, the one named last changes fastest.
Arguments:
- integrals: bfloat16 [4096, 8192], P('tens', 'tile'), may hold values from -1 to 1
- occ_blocks: bfloat16 [64, 64, 256], replicated, may hold values from -0.375 to 0.375
- virt_blocks: bfloat16 [64, 64, 256], replicated, may hold values from -0.375 to 0.375
- occ_partners: int32 [64, 4], replicated, may hold values from 0 to 63
- virt_partners: int32 [64, 4], replicated, may hold values from 0 to 63
- occ_counts: int32 [64], replicated, may hold values from 1 to 4, as said below
- virt_counts: int32 [64], replicated, may hold values from 1 to 4, as said below
Outputs:
- chi_tiles: float32 [8192, 64, 128], P('tile', 'tens')
Inputs may be any that keep to these rules, and one draw needn't show every extreme that they name: `occ_counts`: every draw has one or more pair blocks with all 4 slots in use. `virt_counts`: every draw has one or more pair blocks with all 4 slots in use.
All inputs are finite; a program needn't handle non-finite values.
Results may differ from a plain program's by a relative error of at most 0.0041.
Values may be sent and summed in bfloat16 or wider, within the bound.
No kernel may reach another device: no remote copies, remote signals or barrier semaphores. Data moves between devices by JAX's collectives and lax.ppermute only.
A program may use at most 128 MiB of HBM per device.

v0:
```python
import jax
import jax.numpy as jnp
from jax import lax
from jax.sharding import PartitionSpec as P


def pair_mix(source, partners, counts, blocks):
    block_count = partners.shape[0]
    slot_count = partners.shape[1]
    block_rows = blocks.shape[1]
    width = source.shape[1]
    grouped = source.reshape(block_count, block_rows, width)
    chosen = jnp.take(grouped, partners.reshape(-1), axis=0)
    chosen = chosen.reshape(block_count, slot_count * block_rows, width)
    slot_ids = jnp.arange(slot_count * block_rows, dtype=jnp.int32) // block_rows
    active = (counts[:, None] > slot_ids[None, :]).astype(blocks.dtype)
    weights = blocks * active[:, None, :]
    summed = jnp.einsum("kij,kjp->kip", weights, chosen, preferred_element_type=jnp.float32)
    return summed.reshape(source.shape).astype(jnp.bfloat16)


def on_device(
    integrals, occ_blocks, virt_blocks, occ_partners, virt_partners, occ_counts, virt_counts
):
    columns = lax.all_to_all(integrals, "tens", split_axis=1, concat_axis=0, tiled=True)
    occ_mixed = pair_mix(columns, occ_partners, occ_counts, occ_blocks)
    occ_rows = occ_mixed.T
    tile_source = lax.all_gather(columns, "tile", axis=1, tiled=True)
    virt_tile = pair_mix(tile_source, virt_partners, virt_counts, virt_blocks)
    chi_tile = jnp.dot(
        lax.all_gather(occ_rows, "tens", axis=0, tiled=True),
        virt_tile,
        preferred_element_type=jnp.float32,
    )
    return chi_tile[:, None, :]


def solution(mesh):
    return jax.shard_map(
        on_device,
        mesh=mesh,
        in_specs=(P("tens", "tile"), P(), P(), P(), P(), P(), P()),
        out_specs=P("tile", "tens", None),
        check_vma=False,
    )
```

profile of v0, /device:TPU:8, one launch (start us, length us, event | category | flops | bytes accessed | tf_op | source)
XLA Modules:
  0.0 249.5 jit_solution(16896817492297679595)
XLA Ops:
  6.5 0.0 all-gather.5.cloned.1.call-start
  6.5 1.0 copy.23
  7.5 0.2 reshape.176
  7.7 36.7 %all_to_all.19 = bf16[64,2,256]{2,1,0:T(2,128)(2,1)S(1)} all-to-all(bf16[64,2,256]{2,1,0:T(2,128)(2,1)S(1)} %reshape.176), channel_id=1, replica_groups=mesh['tens'=64,'tile'=16] {'tens'}, dimensions={0} | all-to-all | bytes 131072 | tf_op jit(solution)/shard_map/all_to_all | solution.py:25
  44.4 0.1 reshape.177
  44.6 0.8 all_to_all.17
  45.4 0.0 all-gather.5.cloned.1.call-update
  45.4 0.0 all-gather.3.cloned.1.call-start
  45.4 0.8 copy.24
  46.2 0.1 reshape.157
  46.3 0.7 compare_and_fusion.1
  47.0 0.1 copy.22
  47.1 0.1 broadcast_in_dim.37
  47.3 0.1 broadcast_in_dim.38
  47.4 0.8 compare_convert_fusion
  48.2 0.0 copy-start.2
  48.2 0.8 gather_fusion
  49.0 0.0 copy-start.1
  49.0 0.1 copy.25
  49.1 0.3 gather.13
  49.5 0.3 copy-done.2
  49.8 0.7 fusion.7
  50.5 0.8 convert_element_type.28
  51.3 0.0 all-gather.3.cloned.1.call-update
  51.3 0.0 copy-done.1
  51.3 0.1 copy.31
  51.4 0.1 reshape.159
  51.6 0.1 copy.28
  51.7 0.1 broadcast_in_dim.41
  51.8 0.1 broadcast_in_dim.42
  52.0 29.9 %all-gather.5.cloned.1.call-done = bf16[4096,128]{0,1:T(8,128)(2,1)} async-done(((bf16[4096,8]{0,1:T(8,128)(2,1)}), bf16[4096,128]{0,1:T(8,128)(2,1)}) %all-gather.5.cloned.1.call-update) | async-done | bytes 1048592 | tf_op jit(solution)/shard_map/all_gather | solution.py:28
  81.9 1.6 copy.30
  83.5 3.1 %gather_fusion.1 = bf16[256,64,128]{2,1,0:T(8,128)(2,1)} fusion(bf16[64,64,128]{2,1,0:T(8,128)(2,1)S(1)} %bitcast.28, s32[1024]{0:T(1024)S(1)} %pad_clamp_fusion), kind=kCustom, calls=%fused_computation.1 | custom fusion | bytes 8389632 | tf_op jit(solution)/shard_map/jit(_take)/gather | solution.py:13
  86.6 0.0 copy-start
  86.6 6.2 %bitcast_select_fusion = bf16[64,256,128]{2,1,0:T(8,128)(2,1)S(1)} fusion(pred[64,256]{1,0:T(8,128)(4,1)S(1)} %broadcast_in_dim.42, bf16[64,256,128]{2,1,0:T(8,128)(2,1)} %bitcast.29), kind=kLoop, calls=%fused_computation.2 | loop fusion | flops 2097152 | bytes 8404992 | tf_op jit(solution)/shard_map/jit(_take)/select_n | solution.py:13
  92.7 0.0 copy-done
  92.7 0.9 fusion.4
  93.7 144.9 %all-gather.3.cloned.1.call-done = bf16[512,4096]{1,0:T(8,128)(2,1)} async-done(((bf16[8,4096]{1,0:T(8,128)(2,1)}), bf16[512,4096]{1,0:T(8,128)(2,1)}) %all-gather.3.cloned.1.call-update) | async-done | bytes 4194320 | tf_op jit(solution)/shard_map/all_gather | solution.py:31
  238.6 4.1 %fusion.13 = f32[512,128]{1,0:T(8,128)} fusion(bf16[512,4096]{1,0:T(8,128)(2,1)} %all-gather.3.cloned.1.call-done, bf16[4096,128]{1,0:T(8,128)(2,1)S(1)} %bitcast.30), kind=kOutput, calls=%fused_computation.29 | convolution fusion | flops 536870912 | bytes 5505024 | tf_op jit(solution)/shard_map/dot_general | solution.py:30
  (11 shorter events, 0.1 us)
Async XLA Ops:
  6.5 75.3 %all-gather.5.cloned.1.call-start = ((), (), s32[]{:S(2)}) async-start(), calls=%async_computation.2 | async-start | bytes 1114112 | tf_op jit(solution)/shard_map/all_gather | solution.py:28
  45.4 193.2 %all-gather.3.cloned.1.call-start = ((), (), s32[]{:S(2)}) async-start(), calls=%async_computation.1 | async-start | bytes 4259840 | tf_op jit(solution)/shard_map/all_gather | solution.py:31
  48.2 1.6 copy-start.2
  49.0 2.3 copy-start.1
  86.6 6.2 %copy-start = (bf16[64,64,256]{2,1,0:T(8,128)(2,1)S(1)}, bf16[64,64,256]{2,1,0:T(8,128)(2,1)}, u32[]{:S(2)}) copy-start(bf16[64,64,256]{2,1,0:T(8,128)(2,1)} %param.9) | copy-start | bytes 6291460
Sparse Core Ops, SparseCore 0:
  45.5 36.3 all-gather.4
  86.0 152.5 all-gather.2
where the time goes:
time: 250 us
  waiting for transfers between devices  175 us (70%)
  blocking collectives  36.7 us (15%)
  between operations  13.6 us (5%)
  local copies, waits for them, and re-layouts  10.9 us (4%)
  other arithmetic  7.68 us (3%)
  matrix products  5.73 us (2%)
    all_gather x1, waiting for transfers between devices, on_device(): lax.all_gather(occ_rows, 'tens', axis=0, tiled=True)  145 us
    all_to_all x1, blocking collectives, on_device(): lax.all_to_all(integrals, 'tens', split_axis=1, concat_axis=0, tiled=True)  36.7 us
    all_gather x1, waiting for transfers between devices, on_device(): tile_source = lax.all_gather(columns, 'tile', axis=1, tiled=True)  29.9 us
    select_n x4, other arithmetic, pair_mix(): chosen = jnp.take(grouped, partners.reshape(-1), axis=0)  6.21 us
  transfers between devices with their start and end apart: 2, of which 2 were waited for; matrix products, arithmetic and copies ran while one was open for 7% of the time, Pallas kernels for 0%

commit v1 on v0

v1 whole, which is shorter than its diff:
```python
import functools

import jax
import jax.numpy as jnp
from jax import lax
from jax.experimental import pallas as pl
from jax.experimental.pallas import tpu as pltpu
from jax.sharding import Mesh
from jax.sharding import PartitionSpec as P

NX = 4
NC = 2
BLK = 64
NNZ = 4
QJ = 8
LANES = 128
SUB = 16
FOLD = BLK // SUB
WIDE = FOLD * QJ

VMEM = pl.BlockSpec(memory_space=pltpu.VMEM)
SMEM = pl.BlockSpec(memory_space=pltpu.SMEM)
PARAMS = pltpu.CompilerParams(vmem_limit_bytes=48 * 1024 * 1024)


def lane_ids(rows):
    return lax.broadcasted_iota(jnp.int32, (rows, LANES), 1)


def pack_kernel(raw_ref, out_ref):
    parts = []
    for q in range(FOLD):
        for xs in range(NX):
            piece = raw_ref[q * SUB:(q + 1) * SUB, xs * LANES:(xs + 1) * LANES]
            parts.append(piece.astype(jnp.float32))
    lane_block = lane_ids(SUB) // QJ
    for bit in (1, 2, 4, 8):
        high = (lane_block & bit) != 0
        step = bit * QJ
        swapped = list(parts)
        for m in range(len(parts)):
            if m & bit:
                continue
            low_part, high_part = parts[m], parts[m | bit]
            swapped[m] = jnp.where(high, pltpu.roll(high_part, step, 1), low_part)
            swapped[m | bit] = jnp.where(high, high_part, pltpu.roll(low_part, LANES - step, 1))
        parts = swapped
    for z, part in enumerate(parts):
        value = part.astype(jnp.bfloat16)
        for x in range(NX):
            out_ref[x * len(parts) + z] = value


def mix_kernel(
    part_ref, vp_ref, vc_ref, op_ref, oc_ref, cols_ref, vb_ref, ob_ref, out_ref, spread, mixed, total
):
    blocks = cols_ref.shape[0]
    mine = total.shape[0] - 1
    group = lane_ids(SUB) // WIDE
    first = part_ref[0] * mine

    def widen(k, carry):
        value = cols_ref[k].astype(jnp.float32)
        for q in range(FOLD):
            spread[k, q * SUB:(q + 1) * SUB, :] = jnp.where(group == q, value, 0.0).astype(jnp.bfloat16)
        return carry

    lax.fori_loop(0, blocks, widen, 0, unroll=8)
    spread[blocks] = jnp.zeros(spread.shape[1:], spread.dtype)
    total[...] = jnp.zeros_like(total)

    def virt(k, carry):
        count = vc_ref[k]
        chosen = [
            spread[jnp.where(s < count, vp_ref[s, k], blocks)] for s in range(NNZ)
        ]
        summed = jnp.dot(
            vb_ref[k], jnp.concatenate(chosen, axis=0), preferred_element_type=jnp.float32
        )
        turned = summed.T
        folded = turned[:WIDE]
        for q in range(1, FOLD):
            folded = folded + turned[q * WIDE:(q + 1) * WIDE]
        mixed[k] = folded.astype(jnp.bfloat16)
        return carry

    lax.fori_loop(0, blocks, virt, 0, unroll=8)

    def occ(k, carry):
        count = oc_ref[k]
        spreads = jnp.dot(mixed[k], ob_ref[k], preferred_element_type=jnp.float32)
        for s in range(NNZ):
            half = spreads[:, (s // 2) * LANES:(s // 2 + 1) * LANES]
            if s % 2:
                half = pltpu.roll(half, BLK, 1)
            place = op_ref[s, k] - first
            wanted = (s < count) & (place >= 0) & (place < mine)
            place = jnp.where(wanted, place, mine)
            total[place] = total[place] + half
        return carry

    lax.fori_loop(0, blocks, occ, 0, unroll=8)

    low = lane_ids(WIDE) < BLK
    for a in range(0, mine, 2):
        pair = jnp.where(low, total[a], pltpu.roll(total[a + 1], BLK, 1))
        value = pair.astype(jnp.bfloat16)
        for y in range(out_ref.shape[0]):
            out_ref[y, :, a * BLK:(a + 2) * BLK] = value


def dot_kernel(core_ref, own_ref, other_ref, raw_ref, out_ref):
    first = core_ref[0] == 0
    raw = raw_ref[...]
    for y in range(own_ref.shape[0]):
        own = jnp.dot(own_ref[y], raw, preferred_element_type=jnp.float32)
        other = jnp.dot(other_ref[y], raw, preferred_element_type=jnp.float32)
        zero = jnp.where(first, own, other)
        one = jnp.where(first, other, own)
        for xs in range(NX):
            rows = slice(xs * QJ, (xs + 1) * QJ)
            both = jnp.concatenate([zero[rows], one[rows]], axis=0)
            out_ref[xs, y * SUB:(y + 1) * SUB, :] = both.astype(jnp.bfloat16)


def sum_kernel(parts_ref, out_ref):
    summed = parts_ref[0].astype(jnp.float32)
    for part in range(1, parts_ref.shape[0]):
        summed = summed + parts_ref[part].astype(jnp.float32)
    out_ref[...] = summed.T


def call(kernel, out_shape, dtype, specs, flops, scratch=()):
    return pl.pallas_call(
        kernel,
        out_shape=jax.ShapeDtypeStruct(out_shape, dtype),
        in_specs=specs,
        out_specs=VMEM,
        scratch_shapes=list(scratch),
        compiler_params=PARAMS,
        cost_estimate=pl.CostEstimate(flops=flops, bytes_accessed=1 << 20, transcendentals=0),
    )


def on_device(
    nz, ny, integrals, occ_blocks, virt_blocks, occ_partners, virt_partners, occ_counts, virt_counts
):
    blocks = NX * nz
    width = integrals.shape[1]
    rows = nz * BLK
    raw = lax.all_gather(integrals, "z", axis=0, tiled=True)

    packed = call(pack_kernel, (blocks, SUB, LANES), jnp.bfloat16, [VMEM], 1 << 20)(integrals)
    columns = lax.all_to_all(packed, ("x", "z"), 0, 0, tiled=True)
    copies = call(
        mix_kernel,
        (ny, WIDE, rows),
        jnp.bfloat16,
        [SMEM] * 5 + [VMEM] * 3,
        1 << 28,
        [
            pltpu.VMEM((blocks + 1, BLK, LANES), jnp.bfloat16),
            pltpu.VMEM((blocks, WIDE, BLK), jnp.bfloat16),
            pltpu.VMEM((nz + 1, WIDE, LANES), jnp.float32),
        ],
    )(
        lax.axis_index("x").reshape(1),
        virt_partners.T,
        virt_counts,
        occ_partners.T,
        occ_counts,
        columns,
        virt_blocks,
        occ_blocks,
    )
    own = lax.all_to_all(copies, "y", 0, 0, tiled=True)
    other = lax.ppermute(own, "c", [(0, 1), (1, 0)])
    partial = call(
        dot_kernel,
        (NX, ny * NC * QJ, width),
        jnp.bfloat16,
        [SMEM] + [VMEM] * 3,
        1 << 29,
    )(lax.axis_index("c").reshape(1), own, other, raw)
    parts = lax.all_to_all(partial, "x", 0, 0, tiled=True)
    chi_tile = call(sum_kernel, (width, ny * NC * QJ), jnp.float32, [VMEM], 1 << 20)(parts)
    return chi_tile[:, None, :]


def solution(mesh):
    nz = mesh.shape["tens"] // NX
    ny = mesh.shape["tile"] // NC
    fine = Mesh(mesh.devices.reshape(NX, nz, ny, NC), ("x", "z", "y", "c"))
    return jax.shard_map(
        functools.partial(on_device, nz, ny),
        mesh=fine,
        in_specs=(P(("x", "z"), ("y", "c")), P(), P(), P(), P(), P(), P()),
        out_specs=P(("y", "c"), ("x", "z"), None),
        check_vma=False,
    )
```

time: 250 us -> 134 us (0.54)
  waiting for transfers between devices: 175 us -> 42.9 us
  starting transfers between devices: 0.04 us -> 24.2 us
  Pallas kernels: 0 us -> 11.9 us
  other arithmetic: 7.68 us -> 0 us
  matrix products: 5.73 us -> 0 us
  blocking collectives: 36.7 us -> 33.2 us
  local copies, waits for them, and re-layouts: 10.9 us -> 7.94 us
    all_gather x2 -> x1, waiting for transfers between devices: 175 us -> 21.9 us  [on_device(): raw = lax.all_gather(integrals, 'z', axis=0, tiled=True)]
    all_to_all x0 -> x1, starting transfers between devices: none -> 22.2 us  [on_device(): columns = lax.all_to_all(packed, ('x', 'z'), 0, 0, tiled=True)]
    all_to_all x0 -> x1, waiting for transfers between devices: none -> 20.2 us  [on_device(): columns = lax.all_to_all(packed, ('x', 'z'), 0, 0, tiled=True)]
    pallas_call x0 -> x4, Pallas kernels: none -> 11.9 us  [the longest x1 7.04 us: on_device(): call(mix_kernel, (ny, WIDE, rows), jnp.bfloat16, [SMEM] * 5 + [VMEM] * 3,...]
    select_n x5 -> x0, other arithmetic: 6.22 us -> none  [the longest x4 6.21 us: pair_mix(): chosen = jnp.take(grouped, partners.reshape(-1), axis=0)]
    dot_general x3 -> x0, matrix products: 5.73 us -> none  [the longest x1 4.14 us: on_device(): jnp.dot(lax.all_gather(occ_rows, 'tens', axis=0, tiled=True), virt_tile,...]
    unnamed x12 -> x16, local copies, waits for them, and re-layouts: 2.43 us -> 7.94 us
    gather x4 -> x0, local copies, waits for them, and re-layouts: 4.29 us -> none  [pair_mix(): chosen = jnp.take(grouped, partners.reshape(-1), axis=0)]
  transfers between devices with their start and end apart: 2 -> 3, of which waited for: 2 -> 2; matrix products, arithmetic and copies ran while one was open for 7% -> 0% of each run, Pallas kernels for 0% -> 5%
where the time goes in v1:
time: 134 us
  waiting for transfers between devices  42.9 us (32%)
  blocking collectives  33.2 us (25%)
  starting transfers between devices  24.2 us (18%)
  between operations  13.4 us (10%)
  Pallas kernels  11.9 us (9%)
  local copies, waits for them, and re-layouts  7.94 us (6%)
    all_to_all x1, starting transfers between devices, on_device(): columns = lax.all_to_all(packed, ('x', 'z'), 0, 0, tiled=True)  22.2 us
    all_gather x1, waiting for transfers between devices, on_device(): raw = lax.all_gather(integrals, 'z', axis=0, tiled=True)  21.9 us
    all_to_all x1, blocking collectives, on_device(): own = lax.all_to_all(copies, 'y', 0, 0, tiled=True)  21.2 us
    all_to_all x1, waiting for transfers between devices, on_device(): columns = lax.all_to_all(packed, ('x', 'z'), 0, 0, tiled=True)  20.2 us
    all_to_all x1, blocking collectives, on_device(): parts = lax.all_to_all(partial, 'x', 0, 0, tiled=True)  12.1 us
    unnamed x16, local copies, waits for them, and re-layouts  7.94 us
    pallas_call x1, Pallas kernels, on_device(): call(mix_kernel, (ny, WIDE, rows), jnp.bfloat16, [SMEM] * 5 + [VMEM] * 3,...  7.04 us
    pallas_call x1, Pallas kernels, on_device(): call(dot_kernel, (NX, ny * NC * QJ, width), jnp.bfloat16, [SMEM] + [VMEM]...  3 us
  transfers between devices with their start and end apart: 3, of which 2 were waited for; matrix products, arithmetic and copies ran while one was open for 0% of the time, Pallas kernels for 5%

profile of v1, /device:TPU:8, one launch (start us, length us, event | category | flops | bytes accessed | tf_op | source)
XLA Modules:
  0.0 133.5 jit_solution(10123769067091267434)
XLA Ops:
  6.5 0.0 copy-start.3
  6.5 0.8 copy-done.3
  7.4 1.0 shard_map.73
  8.4 22.2 %all-to-all-start = ((bf16[64,16,128]{2,1,0:T(8,128)(2,1)}), bf16[64,16,128]{2,1,0:T(8,128)(2,1)S(1)}, u32[]{:S(2)}, u32[]{:S(2)}) async-start(bf16[64,16,128]{2,1,0:T(8,128)(2,1)} %shard_map.73), calls=%async_computation | async-start | bytes 524288 | tf_op jit(solution)/shard_map/all_to_all | solution.py:154
  30.6 0.0 all-gather.2.cloned.1.call-start
  30.7 0.7 all-gather.2.cloned.1.call-update
  31.4 20.2 %all-to-all-done.cols_ref = bf16[64,16,128]{2,1,0:T(8,128)(2,1)S(1)} async-done(((bf16[64,16,128]{2,1,0:T(8,128)(2,1)}), bf16[64,16,128]{2,1,0:T(8,128)(2,1)S(1)}, u32[]{:S(2)}, u32[]{:S(2)}) %all-to-all-start) | async-done | bytes 262176 | tf_op jit(solution)/shard_map/all_to_all | solution.py:154
  51.6 0.0 copy-start
  51.6 1.6 %copy-done = bf16[64,64,256]{2,1,0:T(8,128)(2,1)S(1)} copy-done((bf16[64,64,256]{2,1,0:T(8,128)(2,1)S(1)}, bf16[64,64,256]{2,1,0:T(8,128)(2,1)}, u32[]{:S(2)}) %copy-start) | copy-done | bytes 2097176
  53.2 0.0 copy-start.1
  53.2 1.6 %copy-done.1 = bf16[64,64,256]{2,1,0:T(8,128)(2,1)S(1)} copy-done((bf16[64,64,256]{2,1,0:T(8,128)(2,1)S(1)}, bf16[64,64,256]{2,1,0:T(8,128)(2,1)}, u32[]{:S(2)}) %copy-start.1) | copy-done | bytes 2097176
  54.8 0.0 copy-start.4
  54.8 0.7 copy-done.4
  55.5 0.0 copy-start.5
  55.5 0.7 copy-done.5
  56.2 0.0 copy-start.6
  56.2 0.7 copy-done.6
  56.8 0.0 copy-start.7
  56.8 0.7 copy-done.7
  57.5 7.0 %shard_map.74 = bf16[8,32,1024]{2,1,0:T(8,128)(2,1)S(1)} custom-call(s32[1]{0:T(128)} %bitcast.1.part_ref, s32[4,64]{1,0:T(4,128)S(1)} %bitcast.7, s32[64]{0:T(128)S(1)} %copy-done.6, s32[4,64]{1,0:T(4,128)S(1)} %bitcast.8, s32[64]{0:T(128)S(1)} %copy-done.7, bf16[64,16,128]{2,1,0:T(8,128)(2,1)S(1)} %all-to-all-done.cols_ref, ...), custom_call_target="tpu_custom_call" | custom-call | flops 268435456 | bytes 1048576 | tf_op jit(solution)/shard_map/pallas_call | solution.py:155
  64.5 21.2 %all_to_all.15.own_ref = bf16[8,32,1024]{2,1,0:T(8,128)(2,1)S(1)} all-to-all(bf16[8,32,1024]{2,1,0:T(8,128)(2,1)S(1)} %shard_map.74), channel_id=1, replica_groups=mesh['x'=4,'z'=16,'y'=8,'c'=2] {'y'}, dimensions={0} | all-to-all | bytes 1048576 | tf_op jit(solution)/shard_map/all_to_all | solution.py:176
  85.7 1.9 %collective-permute-start = (bf16[8,32,1024]{2,1,0:T(8,128)(2,1)S(1)}, bf16[8,32,1024]{2,1,0:T(8,128)(2,1)S(1)}, u32[]{:S(2)}, u32[]{:S(2)}) collective-permute-start(bf16[8,32,1024]{2,1,0:T(8,128)(2,1)S(1)} %all_to_all.15.own_ref), channel_id=1, source_target_pairs={{0,1},{1,0},{2,3},{3,2},{4,5},{5,4},{6,7},{7,6},{8,9},{9,8},{10,11... | collective-permute-start | bytes 1572872 | tf_op jit(solution)/shard_map/ppermute | solution.py:177
  87.6 21.9 %all-gather.2.cloned.1.call-done.raw_ref = bf16[1024,512]{1,0:T(8,128)(2,1)} async-done(((bf16[64,512]{1,0:T(8,128)(2,1)}), bf16[1024,512]{1,0:T(8,128)(2,1)}) %all-gather.2.cloned.1.call-update) | async-done | bytes 1048592 | tf_op jit(solution)/shard_map/all_gather | solution.py:151
  109.5 0.0 collective-permute-done.other_ref
  109.6 0.0 copy-start.2
  109.6 1.2 copy-done.2
  110.8 3.0 %shard_map.75 = bf16[4,128,512]{2,1,0:T(8,128)(2,1)S(1)} custom-call(s32[1]{0:T(128)} %bitcast.core_ref, bf16[8,32,1024]{2,1,0:T(8,128)(2,1)S(1)} %all_to_all.15.own_ref, bf16[8,32,1024]{2,1,0:T(8,128)(2,1)S(1)} %collective-permute-done.other_ref, bf16[1024,512]{1,0:T(8,128)(2,1)S(1)} %copy-done.2), custom_call_target="tpu_custom_call" | custom-call | flops 536870912 | bytes 1048576 | tf_op jit(solution)/shard_map/pallas_call | solution.py:178
  113.8 12.1 %all_to_all.16.parts_ref = bf16[4,128,512]{2,1,0:T(8,128)(2,1)S(1)} all-to-all(bf16[4,128,512]{2,1,0:T(8,128)(2,1)S(1)} %shard_map.75), channel_id=1, replica_groups=mesh['x'=4,'z'=16,'y'=8,'c'=2] {'x'}, dimensions={0} | all-to-all | bytes 1048576 | tf_op jit(solution)/shard_map/all_to_all | solution.py:185
  125.8 0.8 shard_map.76
Async XLA Ops:
  6.5 0.8 copy-start.3
  8.4 43.2 %all-to-all-start = ((bf16[64,16,128]{2,1,0:T(8,128)(2,1)}), bf16[64,16,128]{2,1,0:T(8,128)(2,1)S(1)}, u32[]{:S(2)}, u32[]{:S(2)}) async-start(bf16[64,16,128]{2,1,0:T(8,128)(2,1)} %shard_map.73), calls=%async_computation | async-start | bytes 524288 | tf_op jit(solution)/shard_map/all_to_all | solution.py:154
  30.6 78.9 %all-gather.2.cloned.1.call-start = ((), (), s32[]{:S(2)}) async-start(), calls=%async_computation.3 | async-start | bytes 1114112 | tf_op jit(solution)/shard_map/all_gather | solution.py:151
  51.6 1.6 %copy-start = (bf16[64,64,256]{2,1,0:T(8,128)(2,1)S(1)}, bf16[64,64,256]{2,1,0:T(8,128)(2,1)}, u32[]{:S(2)}) copy-start(bf16[64,64,256]{2,1,0:T(8,128)(2,1)} %vb_ref.1) | copy-start | bytes 6291460
  53.2 1.6 %copy-start.1 = (bf16[64,64,256]{2,1,0:T(8,128)(2,1)S(1)}, bf16[64,64,256]{2,1,0:T(8,128)(2,1)}, u32[]{:S(2)}) copy-start(bf16[64,64,256]{2,1,0:T(8,128)(2,1)} %ob_ref.1) | copy-start | bytes 6291460
  54.8 0.7 copy-start.4
  55.5 0.7 copy-start.5
  56.2 0.7 copy-start.6
  56.8 0.7 copy-start.7
  85.7 23.8 %collective-permute-start = (bf16[8,32,1024]{2,1,0:T(8,128)(2,1)S(1)}, bf16[8,32,1024]{2,1,0:T(8,128)(2,1)S(1)}, u32[]{:S(2)}, u32[]{:S(2)}) collective-permute-start(bf16[8,32,1024]{2,1,0:T(8,128)(2,1)S(1)} %all_to_all.15.own_ref), channel_id=1, source_target_pairs={{0,1},{1,0},{2,3},{3,2},{4,5},{5,4},{6,7},{7,6},{8,9},{9,8},{10,11... | collective-permute-start | bytes 1572872 | tf_op jit(solution)/shard_map/ppermute | solution.py:177
  109.6 1.2 copy-start.2
Sparse Core Ops, SparseCore 0:
  34.1 75.3 all-gather.1

commit v2 on v0

v2 whole, which is shorter than its diff:
```python
import functools

import jax
import jax.numpy as jnp
from jax import lax
from jax.experimental import pallas as pl
from jax.experimental.pallas import tpu as pltpu
from jax.sharding import Mesh
from jax.sharding import PartitionSpec as P

NX = 4
NC = 2
BLK = 64
NNZ = 4
QJ = 8
LANES = 128
SUB = 16
WIDE = NX * QJ
LATE = 2
HALF = 2
UNROLL = 4

VMEM = pl.BlockSpec(memory_space=pltpu.VMEM)
SMEM = pl.BlockSpec(memory_space=pltpu.SMEM)
PARAMS = pltpu.CompilerParams(vmem_limit_bytes=16 * 1024 * 1024)


def lane_ids(rows):
    return lax.broadcasted_iota(jnp.int32, (rows, LANES), 1)


def pack_kernel(raw_ref, out_ref):
    turned = []
    for xs in range(HALF):
        pair = [raw_ref[:, at * LANES:(at + 1) * LANES] for at in (xs, xs + HALF)]
        turned.append(jnp.concatenate(pair, axis=0).astype(jnp.float32).T)
    last = raw_ref[BLK - SUB:, :].astype(jnp.float32)[SUB - LATE:]
    tail = [
        last[row:row + 1, at:at + LANES] for row in range(LATE) for at in range(0, raw_ref.shape[1], LANES)
    ]
    parts = out_ref.shape[0] // NX
    for z in range(parts):
        rows = [part[z * QJ:(z + 1) * QJ] for part in turned]
        value = jnp.concatenate(rows + tail, axis=0).astype(jnp.bfloat16)
        for x in range(NX):
            out_ref[x * parts + z] = value


def prep_kernel(
    mine, part_ref, vp_ref, vc_ref, op_ref, oc_ref, vb_ref, ob_ref, turned_ref, near_ref, slots_ref
):
    slot = lax.broadcasted_iota(jnp.int32, vp_ref.shape, 0)
    blocks = vp_ref.shape[1]
    slots_ref[:NNZ, :] = jnp.where(slot < vc_ref[...], vp_ref[...], blocks)
    place = op_ref[...] - part_ref[0] * mine
    wanted = (slot < oc_ref[...]) & (place >= 0) & (place < mine)
    slots_ref[NNZ:, :] = jnp.where(wanted, place, mine)

    def turn(pair, carry):
        both = [vb_ref[2 * pair + n].astype(jnp.float32) for n in range(2)]
        turned_ref[pair] = jnp.concatenate(both, axis=0).T.astype(jnp.bfloat16)
        for n in range(2):
            near_ref[pair, n * BLK:(n + 1) * BLK, :] = ob_ref[2 * pair + n]
        return carry

    lax.fori_loop(0, blocks // 2, turn, 0, unroll=4)


def mix_kernel(
    part_ref, slots_ref, cols_ref, vb_ref, ob_ref, out_ref, late_ref, spread, total
):
    blocks = cols_ref.shape[0]
    mine = total.shape[1] - 1
    first = part_ref[0] * mine
    low_sub = lane_ids(SUB) < BLK
    low = lane_ids(WIDE) < BLK
    row = lax.broadcasted_iota(jnp.int32, (2 * WIDE, LANES), 0)
    kept = (row < WIDE) == (lane_ids(2 * WIDE) < BLK)

    def widen(k, carry):
        value = cols_ref[k, :SUB].astype(jnp.float32)
        swapped = pltpu.roll(value, BLK, 1)
        both = [jnp.where(low_sub, value, swapped), jnp.where(low_sub, swapped, value)]
        spread[k] = jnp.concatenate(both, axis=0).astype(jnp.bfloat16)
        return carry

    lax.fori_loop(0, blocks, widen, 0, unroll=8)
    spread[blocks] = jnp.zeros(spread.shape[1:], spread.dtype)
    total[...] = jnp.zeros_like(total)
    for k in range(mine):
        late_ref[k] = cols_ref[first + k, SUB:]

    def chosen(k):
        reads = [spread[slots_ref[s, k]] for s in range(NNZ)]
        return jnp.concatenate(
            [jnp.where(low, reads[s], reads[s + 1]) for s in range(0, NNZ, 2)], axis=1
        )

    def mix(pair, carry):
        lhs = jnp.concatenate([chosen(2 * pair + n) for n in range(2)], axis=0)
        virt = jnp.dot(lhs, vb_ref[pair], preferred_element_type=jnp.float32)
        virt = jnp.where(kept, virt, 0.0).astype(jnp.bfloat16)
        added = jnp.dot(virt, ob_ref[pair], preferred_element_type=jnp.float32)
        for n in range(2):
            for s in range(NNZ):
                place = slots_ref[NNZ + s, 2 * pair + n]
                at = (s // 2) * LANES
                total[s, place] = total[s, place] + added[n * WIDE:(n + 1) * WIDE, at:at + LANES]
        return carry

    lax.fori_loop(0, blocks // 2, mix, 0, unroll=UNROLL)

    for a in range(0, mine, 2):
        even = [total[0, a + n] + total[2, a + n] for n in range(2)]
        odd = [total[1, a + n] + total[3, a + n] for n in range(2)]
        moved = pltpu.roll(jnp.where(low, even[1], odd[0]), BLK, 1)
        value = (jnp.where(low, even[0], odd[1]) + moved).astype(jnp.bfloat16)
        for y in range(out_ref.shape[0]):
            out_ref[y, :, a * BLK:(a + 2) * BLK] = value


def dot_kernel(mixed_ref, early_ref, late_ref, out_ref, raw_ref):
    pairs, width, rows = mixed_ref.shape
    columns = raw_ref.shape[1]
    for k in range(early_ref.shape[0]):
        tail = late_ref[k].astype(jnp.float32)
        step = columns // LANES
        last = [
            jnp.concatenate([tail[row * step + n:row * step + n + 1] for n in range(step)], axis=1)
            for row in range(LATE)
        ]
        block = jnp.concatenate([early_ref[k].astype(jnp.float32), *last], axis=0)
        raw_ref[k * BLK:(k + 1) * BLK, :] = block.astype(jnp.bfloat16)
    summed = jnp.dot(
        mixed_ref[...].reshape(pairs * width, rows), raw_ref[...], preferred_element_type=jnp.float32
    )
    for pair in range(0, pairs, NC):
        for xs in range(NX):
            both = [
                summed[(pair + c) * width + xs * QJ:(pair + c) * width + (xs + 1) * QJ] for c in range(NC)
            ]
            both = jnp.concatenate(both, axis=0).astype(jnp.bfloat16)
            out_ref[xs, pair * QJ:(pair + NC) * QJ, :] = both


def sum_kernel(parts_ref, out_ref):
    summed = parts_ref[0].astype(jnp.float32)
    for part in range(1, parts_ref.shape[0]):
        summed = summed + parts_ref[part].astype(jnp.float32)
    out_ref[...] = summed.T


def call(kernel, outs, specs, flops, scratch=()):
    shapes = [jax.ShapeDtypeStruct(*out) for out in outs]
    single = len(shapes) == 1
    return pl.pallas_call(
        kernel,
        out_shape=shapes[0] if single else shapes,
        in_specs=specs,
        out_specs=VMEM if single else [VMEM] * len(shapes),
        scratch_shapes=list(scratch),
        compiler_params=PARAMS,
        cost_estimate=pl.CostEstimate(flops=flops, bytes_accessed=1 << 20, transcendentals=0),
    )


def on_device(
    nz, ny, integrals, occ_blocks, virt_blocks, occ_partners, virt_partners, occ_counts, virt_counts
):
    blocks = NX * nz
    width = integrals.shape[1]
    rows = nz * BLK
    bf16 = jnp.bfloat16
    early = BLK - LATE
    chunk = SUB + LATE * width // LANES

    packed = call(pack_kernel, [((blocks, chunk, LANES), bf16)], [VMEM], 1 << 20)(integrals)
    columns = lax.all_to_all(packed, ("x", "z"), 0, 0, tiled=True)
    part = lax.axis_index("x").reshape(1)
    virt_near, occ_near, slots = call(
        functools.partial(prep_kernel, nz),
        [
            ((blocks // 2, NNZ * BLK, 2 * BLK), bf16),
            ((blocks // 2, 2 * BLK, NNZ * BLK), bf16),
            ((2 * NNZ, blocks), jnp.int32),
        ],
        [SMEM] + [VMEM] * 6,
        1 << 28,
    )(
        part,
        virt_partners.T,
        virt_counts[None],
        occ_partners.T,
        occ_counts[None],
        virt_blocks,
        occ_blocks,
    )
    copies, raw_late = call(
        mix_kernel,
        [((ny * NC, WIDE, rows), bf16), ((nz, chunk - SUB, LANES), bf16)],
        [SMEM] * 2 + [VMEM] * 3,
        1 << 28,
        [
            pltpu.VMEM((blocks + 1, WIDE, LANES), bf16),
            pltpu.VMEM((NNZ, nz + 1, WIDE, LANES), jnp.float32),
        ],
    )(part, slots, columns, virt_near, occ_near)
    copies, own_rows = lax.optimization_barrier((copies, integrals[:early]))
    raw_early = lax.all_gather(own_rows, "z", axis=0)
    mixed = lax.all_to_all(copies, ("y", "c"), 0, 0, tiled=True)
    mixed, raw_early = lax.optimization_barrier((mixed, raw_early))
    partial = call(
        dot_kernel,
        [((NX, ny * NC * QJ, width), bf16)],
        [VMEM] * 3,
        1 << 29,
        [pltpu.VMEM((rows, width), bf16)],
    )(mixed, raw_early, raw_late)
    parts = lax.all_to_all(partial, "x", 0, 0, tiled=True)
    chi_tile = call(sum_kernel, [((width, ny * NC * QJ), jnp.float32)], [VMEM], 1 << 20)(parts)
    return chi_tile[:, None, :]


def solution(mesh):
    nz = mesh.shape["tens"] // NX
    ny = mesh.shape["tile"] // NC
    fine = Mesh(mesh.devices.reshape(NX, nz, ny, NC), ("x", "z", "y", "c"))
    return jax.shard_map(
        functools.partial(on_device, nz, ny),
        mesh=fine,
        in_specs=(P(("x", "z"), ("y", "c")), P(), P(), P(), P(), P(), P()),
        out_specs=P(("y", "c"), ("x", "z"), None),
        check_vma=False,
    )
```

time: 250 us -> 113 us (0.45)
  the two profiles are of different devices: /device:TPU:8 before, /device:TPU:16 now
where the time goes in v2:
time: 113 us; the launch traced here: 112 us
  blocking collectives  45.4 us (40%)
  starting transfers between devices  29.8 us (26%)
  waiting for transfers between devices  17.9 us (16%)
  local copies, waits for them, and re-layouts  9.61 us (9%)
  Pallas kernels  9.42 us (8%)
    all_gather x1, blocking collectives, on_device(): raw_early = lax.all_gather(own_rows, 'z', axis=0)  33.2 us
    all_to_all x1, starting transfers between devices, on_device(): columns = lax.all_to_all(packed, ('x', 'z'), 0, 0, tiled=True)  22.2 us
    all_to_all x1, waiting for transfers between devices, on_device(): columns = lax.all_to_all(packed, ('x', 'z'), 0, 0, tiled=True)  17.9 us
    all_to_all x1, blocking collectives, on_device(): parts = lax.all_to_all(partial, 'x', 0, 0, tiled=True)  12.1 us
    unnamed x20, local copies, waits for them, and re-layouts  9.61 us
    all_to_all x1, starting transfers between devices, on_device(): mixed = lax.all_to_all(copies, ('y', 'c'), 0, 0, tiled=True)  7.58 us
    pallas_call x1, Pallas kernels, on_device(): call(mix_kernel, [((ny * NC, WIDE, rows), bf16), ((nz, chunk - SUB, LANES...  5.78 us
  transfers between devices with their start and end apart: 2, of which 1 were waited for; matrix products, arithmetic and copies ran while one was open for 0% of the time, Pallas kernels for 1%

profile of v2, /device:TPU:16, one launch (start us, length us, event | category | flops | bytes accessed | tf_op | source)
XLA Modules:
  0.0 112.2 jit_solution(12804786922311122604)
XLA Ops:
  0.0 0.0 copy-start.4
  0.0 0.8 copy-done.4
  0.8 0.8 shard_map.74
  1.7 22.2 %all-to-all-start = ((bf16[64,24,128]{2,1,0:T(8,128)(2,1)}), bf16[64,24,128]{2,1,0:T(8,128)(2,1)S(1)}, u32[]{:S(2)}, u32[]{:S(2)}) async-start(bf16[64,24,128]{2,1,0:T(8,128)(2,1)} %shard_map.74), calls=%async_computation | async-start | bytes 786432 | tf_op jit(solution)/shard_map/all_to_all | solution.py:178
  23.9 0.0 copy-start
  23.9 1.6 %copy-done = bf16[64,64,256]{2,1,0:T(8,128)(2,1)S(1)} copy-done((bf16[64,64,256]{2,1,0:T(8,128)(2,1)S(1)}, bf16[64,64,256]{2,1,0:T(8,128)(2,1)}, u32[]{:S(2)}) %copy-start) | copy-done | bytes 2097176
  25.5 0.0 copy-start.1
  25.5 1.6 %copy-done.1 = bf16[64,64,256]{2,1,0:T(8,128)(2,1)S(1)} copy-done((bf16[64,64,256]{2,1,0:T(8,128)(2,1)S(1)}, bf16[64,64,256]{2,1,0:T(8,128)(2,1)}, u32[]{:S(2)}) %copy-start.1) | copy-done | bytes 2097176
  27.1 0.0 copy-start.6
  27.1 0.7 copy-done.6
  27.8 0.0 copy-start.7
  27.8 0.7 copy-done.7
  28.5 0.0 copy-start.8
  28.5 0.7 copy-done.8
  29.1 0.0 copy-start.9
  29.1 0.7 copy-done.9
  29.8 1.2 %shard_map.73 = (bf16[32,256,128]{2,1,0:T(8,128)(2,1)S(1)}, bf16[32,128,256]{2,1,0:T(8,128)(2,1)S(1)}, s32[8,64]{1,0:T(8,128)S(1)}) custom-call(s32[1]{0:T(128)} %bitcast.part_ref, s32[4,64]{1,0:T(4,128)S(1)} %bitcast.11, s32[1,64]{1,0:T(1,128)S(1)} %bitcast.13, s32[4,64]{1,0:T(4,128)S(1)} %bitcast.12, s32[1,64]{1,0:T(1,128)S(1)} %bitcast.14, ...), custom_call_target="tpu_custom_call" | custom-call | flops 268435456 | bytes 1048576 | tf_op jit(solution)/shard_map/pallas_call | solution.py:180
  31.0 0.0 copy-start.2
  31.0 1.3 %copy-done.2 = bf16[32,128,256]{2,1,0:T(8,128)(2,1)} copy-done((bf16[32,128,256]{2,1,0:T(8,128)(2,1)}, bf16[32,128,256]{2,1,0:T(8,128)(2,1)S(1)}, u32[]{:S(2)}) %copy-start.2) | copy-done | bytes 2097176
  32.4 17.9 %all-to-all-done.cols_ref = bf16[64,24,128]{2,1,0:T(8,128)(2,1)S(1)} async-done(((bf16[64,24,128]{2,1,0:T(8,128)(2,1)}), bf16[64,24,128]{2,1,0:T(8,128)(2,1)S(1)}, u32[]{:S(2)}, u32[]{:S(2)}) %all-to-all-start) | async-done | bytes 393248 | tf_op jit(solution)/shard_map/all_to_all | solution.py:178
  50.3 0.0 copy-start.3
  50.3 1.6 %copy-done.3 = bf16[32,128,256]{2,1,0:T(8,128)(2,1)S(1)} copy-done((bf16[32,128,256]{2,1,0:T(8,128)(2,1)S(1)}, bf16[32,128,256]{2,1,0:T(8,128)(2,1)}, u32[]{:S(2)}) %copy-start.3) | copy-done | bytes 2097176
  51.9 5.8 %shard_map.75 = (bf16[16,32,1024]{2,1,0:T(8,128)(2,1)}, bf16[16,8,128]{2,1,0:T(8,128)(2,1)S(1)}) custom-call(s32[1]{0:T(128)} %bitcast.part_ref, s32[8,64]{1,0:T(8,128)S(1)} %get-tuple-element.14.slots_ref, bf16[64,24,128]{2,1,0:T(8,128)(2,1)S(1)} %all-to-all-done.cols_ref, bf16[32,256,128]{2,1,0:T(8,128)(2,1)S(1)} %get-tuple-element.15.vb_ref, ...), custom_call_target="tpu_custom_call" | custom-call | flops 268435456 | bytes 1048576 | tf_op jit(solution)/shard_map/pallas_call | solution.py:198
  57.7 0.0 copy-start.5
  57.7 7.6 %all-to-all-start.1 = ((bf16[16,32,1024]{2,1,0:T(8,128)(2,1)}), bf16[16,32,1024]{2,1,0:T(8,128)(2,1)S(1)}, u32[]{:S(2)}, u32[]{:S(2)}) async-start(bf16[16,32,1024]{2,1,0:T(8,128)(2,1)} %get-tuple-element.18), calls=%async_computation.1 | async-start | bytes 2097152 | tf_op jit(solution)/shard_map/all_to_all | solution.py:210
  65.2 0.0 copy-done.5
  65.2 33.2 %all-gather.1.early_ref = bf16[16,62,512]{2,1,0:T(8,128)(2,1)S(1)} all-gather(bf16[1,62,512]{2,1,0:T(8,128)(2,1)S(1)} %bitcast.10), channel_id=2, replica_groups=mesh['x'=4,'z'=16,'y'=8,'c'=2] {'z'}, dimensions={0}, use_global_device_ids=true | all-gather | bytes 1079296 | tf_op jit(solution)/shard_map/all_gather | solution.py:209
  98.5 0.0 all-to-all-done.1.mixed_ref
  98.5 0.7 shard_map.76
  99.2 12.1 %all_to_all.15.parts_ref = bf16[4,128,512]{2,1,0:T(8,128)(2,1)S(1)} all-to-all(bf16[4,128,512]{2,1,0:T(8,128)(2,1)S(1)} %shard_map.76), channel_id=1, replica_groups=mesh['x'=4,'z'=16,'y'=8,'c'=2] {'x'}, dimensions={0} | all-to-all | bytes 1048576 | tf_op jit(solution)/shard_map/all_to_all | solution.py:219
  111.3 0.8 shard_map.77
Async XLA Ops:
  0.0 0.8 copy-start.4
  1.7 48.6 %all-to-all-start = ((bf16[64,24,128]{2,1,0:T(8,128)(2,1)}), bf16[64,24,128]{2,1,0:T(8,128)(2,1)S(1)}, u32[]{:S(2)}, u32[]{:S(2)}) async-start(bf16[64,24,128]{2,1,0:T(8,128)(2,1)} %shard_map.74), calls=%async_computation | async-start | bytes 786432 | tf_op jit(solution)/shard_map/all_to_all | solution.py:178
  23.9 1.6 %copy-start = (bf16[64,64,256]{2,1,0:T(8,128)(2,1)S(1)}, bf16[64,64,256]{2,1,0:T(8,128)(2,1)}, u32[]{:S(2)}) copy-start(bf16[64,64,256]{2,1,0:T(8,128)(2,1)} %vb_ref.1) | copy-start | bytes 6291460
  25.5 1.6 %copy-start.1 = (bf16[64,64,256]{2,1,0:T(8,128)(2,1)S(1)}, bf16[64,64,256]{2,1,0:T(8,128)(2,1)}, u32[]{:S(2)}) copy-start(bf16[64,64,256]{2,1,0:T(8,128)(2,1)} %ob_ref.1) | copy-start | bytes 6291460
  27.1 0.7 copy-start.6
  27.8 0.7 copy-start.7
  28.5 0.7 copy-start.8
  29.1 0.7 copy-start.9
  31.0 1.3 %copy-start.2 = (bf16[32,128,256]{2,1,0:T(8,128)(2,1)}, bf16[32,128,256]{2,1,0:T(8,128)(2,1)S(1)}, u32[]{:S(2)}) copy-start(bf16[32,128,256]{2,1,0:T(8,128)(2,1)S(1)} %get-tuple-element.16.ob_ref) | copy-start | bytes 6291460
  50.3 1.6 %copy-start.3 = (bf16[32,128,256]{2,1,0:T(8,128)(2,1)S(1)}, bf16[32,128,256]{2,1,0:T(8,128)(2,1)}, u32[]{:S(2)}) copy-start(bf16[32,128,256]{2,1,0:T(8,128)(2,1)} %copy-done.2) | copy-start | bytes 6291460
  57.7 7.6 %copy-start.5 = (bf16[64,512]{1,0:T(8,128)(2,1)S(1)}, bf16[64,512]{1,0:T(8,128)(2,1)}, u32[]{:S(2)}) copy-start(bf16[64,512]{1,0:T(8,128)(2,1)} %raw_ref.1) | copy-start | bytes 196612
  57.7 40.8 %all-to-all-start.1 = ((bf16[16,32,1024]{2,1,0:T(8,128)(2,1)}), bf16[16,32,1024]{2,1,0:T(8,128)(2,1)S(1)}, u32[]{:S(2)}, u32[]{:S(2)}) async-start(bf16[16,32,1024]{2,1,0:T(8,128)(2,1)} %get-tuple-element.18), calls=%async_computation.1 | async-start | bytes 2097152 | tf_op jit(solution)/shard_map/all_to_all | solution.py:210

commit v3 on v2

v3 whole, which is shorter than its diff:
```python
import functools

import jax
import jax.numpy as jnp
from jax import lax
from jax.experimental import pallas as pl
from jax.experimental.pallas import tpu as pltpu
from jax.sharding import Mesh
from jax.sharding import PartitionSpec as P

NX = 4
NC = 2
BLK = 64
NNZ = 4
QJ = 8
LANES = 128
SUB = 16
LATE = 2
UNROLL = 16

VMEM = pl.BlockSpec(memory_space=pltpu.VMEM)
SMEM = pl.BlockSpec(memory_space=pltpu.SMEM)
PARAMS = pltpu.CompilerParams(vmem_limit_bytes=16 * 1024 * 1024)


def lane_ids(rows):
    return lax.broadcasted_iota(jnp.int32, (rows, LANES), 1)


def pack_kernel(raw_ref, out_ref):
    last = raw_ref[BLK - SUB:, :].astype(jnp.float32)[SUB - LATE:]
    tail = [
        last[row:row + 1, at:at + LANES] for row in range(LATE) for at in range(0, raw_ref.shape[1], LANES)
    ]
    parts = out_ref.shape[0] // NX
    for x in range(NX):
        piece = raw_ref[:, x * LANES:(x + 1) * LANES]
        turned = jnp.concatenate([piece, piece], axis=0).astype(jnp.float32).T
        for z in range(parts):
            value = jnp.concatenate([turned[z * QJ:(z + 1) * QJ], *tail], axis=0)
            out_ref[x * parts + z] = value.astype(jnp.bfloat16)


def prep_kernel(vp_ref, vc_ref, op_ref, oc_ref, vb_ref, ob_ref, turned_ref, near_ref, slots_ref):
    slot = lax.broadcasted_iota(jnp.int32, vp_ref.shape, 0)
    blocks = vp_ref.shape[1]
    slots_ref[:NNZ, :] = jnp.where(slot < vc_ref[...], vp_ref[...], blocks)
    slots_ref[NNZ:, :] = jnp.where(slot < oc_ref[...], op_ref[...], blocks)

    def turn(pair, carry):
        both = [vb_ref[2 * pair + n].astype(jnp.float32) for n in range(2)]
        turned_ref[pair] = jnp.concatenate(both, axis=0).T.astype(jnp.bfloat16)
        for n in range(2):
            near_ref[pair, n * BLK:(n + 1) * BLK, :] = ob_ref[2 * pair + n]
        return carry

    lax.fori_loop(0, blocks // 2, turn, 0, unroll=4)


def mix_kernel(slots_ref, cols_ref, vb_ref, ob_ref, out_ref, spread, total):
    blocks = cols_ref.shape[0]
    part = out_ref.shape[2] // BLK
    copies = out_ref.shape[0] * part // blocks
    low = lane_ids(SUB) < BLK
    low_out = lane_ids(QJ) < BLK
    row = lax.broadcasted_iota(jnp.int32, (2 * SUB, LANES), 0)
    kept = ((row < SUB) == (lane_ids(2 * SUB) < BLK)) & ((row & (SUB - 1)) < QJ)

    spread[:blocks] = cols_ref[...]
    spread[blocks] = jnp.zeros(spread.shape[1:], spread.dtype)
    total[...] = jnp.zeros_like(total)

    def chosen(k):
        reads = [spread[slots_ref[s, k]] for s in range(NNZ)]
        return jnp.concatenate(
            [jnp.where(low, reads[s], reads[s + 1]) for s in range(0, NNZ, 2)], axis=1
        )

    def mix(pair, carry):
        lhs = jnp.concatenate([chosen(2 * pair + n) for n in range(2)], axis=0)
        virt = jnp.dot(lhs, vb_ref[pair], preferred_element_type=jnp.float32)
        virt = jnp.where(kept, virt, 0.0).astype(jnp.bfloat16)
        added = jnp.dot(virt, ob_ref[pair], preferred_element_type=jnp.float32)
        for n in range(2):
            for s in range(NNZ):
                place = slots_ref[NNZ + s, 2 * pair + n]
                at = (s // 2) * LANES
                total[s, place] = total[s, place] + added[n * SUB:n * SUB + QJ, at:at + LANES]
        return carry

    lax.fori_loop(0, blocks // 2, mix, 0, unroll=UNROLL)

    for a in range(0, blocks, 2):
        even = [total[0, a + n] + total[2, a + n] for n in range(2)]
        odd = [total[1, a + n] + total[3, a + n] for n in range(2)]
        moved = pltpu.roll(jnp.where(low_out, even[1], odd[0]), BLK, 1)
        value = (jnp.where(low_out, even[0], odd[1]) + moved).astype(jnp.bfloat16)
        at = a % part * BLK
        for copy in range(copies):
            out_ref[a // part * copies + copy, :, at:at + LANES] = value


def dot_kernel(part_ref, mixed_ref, early_ref, cols_ref, out_ref, raw_ref):
    part = early_ref.shape[0]
    step = raw_ref.shape[1] // LANES
    for k in range(part):
        tail = cols_ref[part_ref[0] * part + k].astype(jnp.float32)[QJ:]
        last = [
            jnp.concatenate([tail[row * step + n:row * step + n + 1] for n in range(step)], axis=1)
            for row in range(LATE)
        ]
        block = jnp.concatenate([early_ref[k].astype(jnp.float32), *last], axis=0)
        raw_ref[k * BLK:(k + 1) * BLK, :] = block.astype(jnp.bfloat16)
    summed = jnp.dot(mixed_ref[...], raw_ref[...], preferred_element_type=jnp.float32)
    out_ref[...] = summed.astype(jnp.bfloat16)


def sum_kernel(parts_ref, out_ref):
    summed = parts_ref[0].astype(jnp.float32)
    for part in range(1, parts_ref.shape[0]):
        summed = summed + parts_ref[part].astype(jnp.float32)
    out_ref[...] = summed.T


def call(kernel, outs, specs, flops, scratch=()):
    shapes = [jax.ShapeDtypeStruct(*out) for out in outs]
    single = len(shapes) == 1
    return pl.pallas_call(
        kernel,
        out_shape=shapes[0] if single else shapes,
        in_specs=specs,
        out_specs=VMEM if single else [VMEM] * len(shapes),
        scratch_shapes=list(scratch),
        compiler_params=PARAMS,
        cost_estimate=pl.CostEstimate(flops=flops, bytes_accessed=1 << 20, transcendentals=0),
    )


def on_device(
    nz, ny, integrals, occ_blocks, virt_blocks, occ_partners, virt_partners, occ_counts, virt_counts
):
    blocks = NX * nz
    width = integrals.shape[1]
    rows = nz * BLK
    bf16 = jnp.bfloat16
    early = BLK - LATE
    peers = NX * ny * NC

    packed = call(pack_kernel, [((blocks, SUB, LANES), bf16)], [VMEM], 1 << 20)(integrals)
    columns = lax.all_to_all(packed, ("x", "z"), 0, 0, tiled=True)
    virt_near, occ_near, slots = call(
        prep_kernel,
        [
            ((blocks // 2, NNZ * BLK, 2 * BLK), bf16),
            ((blocks // 2, 2 * BLK, NNZ * BLK), bf16),
            ((2 * NNZ, blocks), jnp.int32),
        ],
        [VMEM] * 6,
        1 << 28,
    )(
        virt_partners.T,
        virt_counts[None],
        occ_partners.T,
        occ_counts[None],
        virt_blocks,
        occ_blocks,
    )
    copies = call(
        mix_kernel,
        [((peers, QJ, rows), bf16)],
        [SMEM] + [VMEM] * 3,
        1 << 28,
        [
            pltpu.VMEM((blocks + 1, SUB, LANES), bf16),
            pltpu.VMEM((NNZ, blocks + 1, QJ, LANES), jnp.float32),
        ],
    )(slots, columns, virt_near, occ_near)
    copies, own_rows = lax.optimization_barrier((copies, integrals[:early]))
    raw_early = lax.all_gather(own_rows, "z", axis=0)
    mixed = lax.all_to_all(copies, ("x", "y", "c"), 0, 0, tiled=True)
    mixed, raw_early = lax.optimization_barrier((mixed, raw_early))
    partial = call(
        dot_kernel,
        [((peers * QJ, width), bf16)],
        [SMEM] + [VMEM] * 3,
        1 << 29,
        [pltpu.VMEM((rows, width), bf16)],
    )(lax.axis_index("x").reshape(1), mixed.reshape(peers * QJ, rows), raw_early, columns)
    partial = partial.reshape(NX, ny * NC * QJ, width)
    parts = lax.all_to_all(partial, "x", 0, 0, tiled=True)
    chi_tile = call(sum_kernel, [((width, ny * NC * QJ), jnp.float32)], [VMEM], 1 << 20)(parts)
    return chi_tile[:, None, :]


def solution(mesh):
    nz = mesh.shape["tens"] // NX
    ny = mesh.shape["tile"] // NC
    fine = Mesh(mesh.devices.reshape(NX, nz, ny, NC), ("x", "z", "y", "c"))
    return jax.shard_map(
        functools.partial(on_device, nz, ny),
        mesh=fine,
        in_specs=(P(("x", "z"), ("y", "c")), P(), P(), P(), P(), P(), P()),
        out_specs=P(("y", "c"), ("x", "z"), None),
        check_vma=False,
    )
```

time: 113 us -> 108 us (0.956)
  the two profiles are of different devices: /device:TPU:16 before, /device:TPU:8 now
where the time goes in v3:
time: 108 us
  blocking collectives  45.2 us (42%)
  starting transfers between devices  32.9 us (30%)
  waiting for transfers between devices  12.5 us (12%)
  local copies, waits for them, and re-layouts  9.61 us (9%)
  Pallas kernels  7.28 us (7%)
    all_gather x1, blocking collectives, on_device(): raw_early = lax.all_gather(own_rows, 'z', axis=0)  33 us
    all_to_all x1, starting transfers between devices, on_device(): columns = lax.all_to_all(packed, ('x', 'z'), 0, 0, tiled=True)  22.2 us
    all_to_all x1, waiting for transfers between devices, on_device(): columns = lax.all_to_all(packed, ('x', 'z'), 0, 0, tiled=True)  12.5 us
    all_to_all x1, blocking collectives, on_device(): parts = lax.all_to_all(partial, 'x', 0, 0, tiled=True)  12.2 us
    all_to_all x1, starting transfers between devices, on_device(): mixed = lax.all_to_all(copies, ('x', 'y', 'c'), 0, 0, tiled=True)  10.7 us
    unnamed x20, local copies, waits for them, and re-layouts  9.61 us
    pallas_call x1, Pallas kernels, on_device(): call(mix_kernel, [((peers, QJ, rows), bf16)], [SMEM] + [VMEM] * 3, 1 << 2...  3.69 us
  transfers between devices with their start and end apart: 2, of which 1 were waited for; matrix products, arithmetic and copies ran while one was open for 0% of the time, Pallas kernels for 1%

profile of v3, /device:TPU:8, one launch (start us, length us, event | category | flops | bytes accessed | tf_op | source)
XLA Modules:
  0.0 107.7 jit_solution(13560606006260114220)
XLA Ops:
  0.0 0.0 copy-start.4
  0.0 0.8 copy-done.4
  0.8 0.8 shard_map.74
  1.6 22.2 %all-to-all-start = ((bf16[64,16,128]{2,1,0:T(8,128)(2,1)}), bf16[64,16,128]{2,1,0:T(8,128)(2,1)S(1)}, u32[]{:S(2)}, u32[]{:S(2)}) async-start(bf16[64,16,128]{2,1,0:T(8,128)(2,1)} %shard_map.74), calls=%async_computation | async-start | bytes 524288 | tf_op jit(solution)/shard_map/all_to_all | solution.py:150
  23.9 0.0 copy-start
  23.9 1.6 %copy-done = bf16[64,64,256]{2,1,0:T(8,128)(2,1)S(1)} copy-done((bf16[64,64,256]{2,1,0:T(8,128)(2,1)S(1)}, bf16[64,64,256]{2,1,0:T(8,128)(2,1)}, u32[]{:S(2)}) %copy-start) | copy-done | bytes 2097176
  25.5 0.0 copy-start.1
  25.5 1.6 %copy-done.1 = bf16[64,64,256]{2,1,0:T(8,128)(2,1)S(1)} copy-done((bf16[64,64,256]{2,1,0:T(8,128)(2,1)S(1)}, bf16[64,64,256]{2,1,0:T(8,128)(2,1)}, u32[]{:S(2)}) %copy-start.1) | copy-done | bytes 2097176
  27.1 0.0 copy-start.6
  27.1 0.7 copy-done.6
  27.8 0.0 copy-start.7
  27.8 0.7 copy-done.7
  28.4 0.0 copy-start.8
  28.4 0.7 copy-done.8
  29.1 0.0 copy-start.9
  29.1 0.7 copy-done.9
  29.7 1.2 %shard_map.73 = (bf16[32,256,128]{2,1,0:T(8,128)(2,1)S(1)}, bf16[32,128,256]{2,1,0:T(8,128)(2,1)S(1)}, s32[8,64]{1,0:T(8,128)S(1)}) custom-call(s32[4,64]{1,0:T(4,128)S(1)} %bitcast.15, s32[1,64]{1,0:T(1,128)S(1)} %bitcast.17, s32[4,64]{1,0:T(4,128)S(1)} %bitcast.16, s32[1,64]{1,0:T(1,128)S(1)} %bitcast.18, bf16[64,64,256]{2,1,0:T(8,128)(2,1)S(1)} %copy-done, ...), custom_call_target="tpu_custom_call" | custom-call | flops 268435456 | bytes 1048576 | tf_op jit(solution)/shard_map/pallas_call | solution.py:151
  31.0 0.0 copy-start.2
  31.0 1.3 %copy-done.2 = bf16[32,128,256]{2,1,0:T(8,128)(2,1)} copy-done((bf16[32,128,256]{2,1,0:T(8,128)(2,1)}, bf16[32,128,256]{2,1,0:T(8,128)(2,1)S(1)}, u32[]{:S(2)}) %copy-start.2) | copy-done | bytes 2097176
  32.3 12.5 %all-to-all-done.cols_ref = bf16[64,16,128]{2,1,0:T(8,128)(2,1)S(1)} async-done(((bf16[64,16,128]{2,1,0:T(8,128)(2,1)}), bf16[64,16,128]{2,1,0:T(8,128)(2,1)S(1)}, u32[]{:S(2)}, u32[]{:S(2)}) %all-to-all-start) | async-done | bytes 262176 | tf_op jit(solution)/shard_map/all_to_all | solution.py:150
  44.9 0.0 copy-start.3
  44.9 1.6 %copy-done.3 = bf16[32,128,256]{2,1,0:T(8,128)(2,1)S(1)} copy-done((bf16[32,128,256]{2,1,0:T(8,128)(2,1)S(1)}, bf16[32,128,256]{2,1,0:T(8,128)(2,1)}, u32[]{:S(2)}) %copy-start.3) | copy-done | bytes 2097176
  46.5 3.7 %shard_map.75 = bf16[64,8,1024]{2,1,0:T(8,128)(2,1)} custom-call(s32[8,64]{1,0:T(8,128)S(1)} %get-tuple-element.12.slots_ref, bf16[64,16,128]{2,1,0:T(8,128)(2,1)S(1)} %all-to-all-done.cols_ref, bf16[32,256,128]{2,1,0:T(8,128)(2,1)S(1)} %get-tuple-element.13.vb_ref, bf16[32,128,256]{2,1,0:T(8,128)(2,1)S(1)} %copy-done.3), custom_call_target="tpu_custom_call" | custom-call | flops 268435456 | bytes 1048576 | tf_op jit(solution)/shard_map/pallas_call | solution.py:168
  50.2 0.0 copy-start.5
  50.2 10.7 %all-to-all-start.1 = ((bf16[64,8,1024]{2,1,0:T(8,128)(2,1)}), bf16[64,8,1024]{2,1,0:T(8,128)(2,1)S(1)}, u32[]{:S(2)}, u32[]{:S(2)}) async-start(bf16[64,8,1024]{2,1,0:T(8,128)(2,1)} %shard_map.75), calls=%async_computation.1 | async-start | bytes 2097152 | tf_op jit(solution)/shard_map/all_to_all | solution.py:180
  60.8 0.0 copy-done.5
  60.9 33.0 %all-gather.1.early_ref = bf16[16,62,512]{2,1,0:T(8,128)(2,1)S(1)} all-gather(bf16[1,62,512]{2,1,0:T(8,128)(2,1)S(1)} %bitcast.14), channel_id=2, replica_groups=mesh['x'=4,'z'=16,'y'=8,'c'=2] {'z'}, dimensions={0}, use_global_device_ids=true | all-gather | bytes 1079296 | tf_op jit(solution)/shard_map/all_gather | solution.py:179
  93.9 0.0 all-to-all-done.1
  93.9 0.7 shard_map.76
  94.6 12.2 %all_to_all.15.parts_ref = bf16[4,128,512]{2,1,0:T(8,128)(2,1)S(1)} all-to-all(bf16[4,128,512]{2,1,0:T(8,128)(2,1)S(1)} %bitcast.13), channel_id=1, replica_groups=mesh['x'=4,'z'=16,'y'=8,'c'=2] {'x'}, dimensions={0} | all-to-all | bytes 1048576 | tf_op jit(solution)/shard_map/all_to_all | solution.py:190
  106.8 0.8 shard_map.77
Async XLA Ops:
  0.0 0.8 copy-start.4
  1.6 43.2 %all-to-all-start = ((bf16[64,16,128]{2,1,0:T(8,128)(2,1)}), bf16[64,16,128]{2,1,0:T(8,128)(2,1)S(1)}, u32[]{:S(2)}, u32[]{:S(2)}) async-start(bf16[64,16,128]{2,1,0:T(8,128)(2,1)} %shard_map.74), calls=%async_computation | async-start | bytes 524288 | tf_op jit(solution)/shard_map/all_to_all | solution.py:150
  23.9 1.6 %copy-start = (bf16[64,64,256]{2,1,0:T(8,128)(2,1)S(1)}, bf16[64,64,256]{2,1,0:T(8,128)(2,1)}, u32[]{:S(2)}) copy-start(bf16[64,64,256]{2,1,0:T(8,128)(2,1)} %vb_ref.1) | copy-start | bytes 6291460
  25.5 1.6 %copy-start.1 = (bf16[64,64,256]{2,1,0:T(8,128)(2,1)S(1)}, bf16[64,64,256]{2,1,0:T(8,128)(2,1)}, u32[]{:S(2)}) copy-start(bf16[64,64,256]{2,1,0:T(8,128)(2,1)} %ob_ref.1) | copy-start | bytes 6291460
  27.1 0.7 copy-start.6
  27.8 0.7 copy-start.7
  28.4 0.7 copy-start.8
  29.1 0.7 copy-start.9
  31.0 1.3 %copy-start.2 = (bf16[32,128,256]{2,1,0:T(8,128)(2,1)}, bf16[32,128,256]{2,1,0:T(8,128)(2,1)S(1)}, u32[]{:S(2)}) copy-start(bf16[32,128,256]{2,1,0:T(8,128)(2,1)S(1)} %get-tuple-element.14.ob_ref) | copy-start | bytes 6291460
  44.9 1.6 %copy-start.3 = (bf16[32,128,256]{2,1,0:T(8,128)(2,1)S(1)}, bf16[32,128,256]{2,1,0:T(8,128)(2,1)}, u32[]{:S(2)}) copy-start(bf16[32,128,256]{2,1,0:T(8,128)(2,1)} %copy-done.2) | copy-start | bytes 6291460
  50.2 10.7 %copy-start.5 = (bf16[64,512]{1,0:T(8,128)(2,1)S(1)}, bf16[64,512]{1,0:T(8,128)(2,1)}, u32[]{:S(2)}) copy-start(bf16[64,512]{1,0:T(8,128)(2,1)} %raw_ref.1) | copy-start | bytes 196612
  50.2 43.7 %all-to-all-start.1 = ((bf16[64,8,1024]{2,1,0:T(8,128)(2,1)}), bf16[64,8,1024]{2,1,0:T(8,128)(2,1)S(1)}, u32[]{:S(2)}, u32[]{:S(2)}) async-start(bf16[64,8,1024]{2,1,0:T(8,128)(2,1)} %shard_map.75), calls=%async_computation.1 | async-start | bytes 2097152 | tf_op jit(solution)/shard_map/all_to_all | solution.py:180

commit v4 on v3

v4 whole, which is shorter than its diff:
```python
import functools

import jax
import jax.numpy as jnp
from jax import lax
from jax.experimental import pallas as pl
from jax.experimental.pallas import tpu as pltpu
from jax.sharding import Mesh
from jax.sharding import PartitionSpec as P

NX = 4
NC = 2
BLK = 64
NNZ = 4
QJ = 8
LANES = 128
SUB = 16
UNROLL = 16

VMEM = pl.BlockSpec(memory_space=pltpu.VMEM)
SMEM = pl.BlockSpec(memory_space=pltpu.SMEM)
LIMIT = 16 * 1024 * 1024


def lane_ids(rows):
    return lax.broadcasted_iota(jnp.int32, (rows, LANES), 1)


def pack_kernel(raw_ref, out_ref, early_ref):
    early_ref[...] = raw_ref[:early_ref.shape[0], :]
    last = raw_ref[BLK - SUB:, :].astype(jnp.float32)[SUB - 1:]
    pieces = []
    for at in range(0, raw_ref.shape[1], LANES):
        piece = last[:, at:at + LANES]
        pieces += [pltpu.roll(piece, BLK, 1), piece]
    tail = jnp.concatenate(pieces, axis=0)
    low = lane_ids(QJ) < BLK
    parts = out_ref.shape[0] // NX
    for x in range(NX):
        piece = raw_ref[:, x * LANES:(x + 1) * LANES]
        turned = jnp.concatenate([piece, piece], axis=0).astype(jnp.float32).T
        for z in range(parts):
            value = jnp.where(low, turned[z * QJ:(z + 1) * QJ], tail)
            out_ref[x * parts + z] = value.astype(jnp.bfloat16)


def prep_kernel(vp_ref, vc_ref, op_ref, oc_ref, vb_ref, turned_ref, slots_ref):
    slot = lax.broadcasted_iota(jnp.int32, vp_ref.shape, 0)
    blocks = vp_ref.shape[1]
    slots_ref[:NNZ, :] = jnp.where(slot < vc_ref[...], vp_ref[...], blocks)
    slots_ref[NNZ:, :] = jnp.where(slot < oc_ref[...], op_ref[...], blocks)

    def turn(pair, carry):
        both = [vb_ref[2 * pair + n].astype(jnp.float32) for n in range(2)]
        turned_ref[pair] = jnp.concatenate(both, axis=0).T.astype(jnp.bfloat16)
        return carry

    lax.fori_loop(0, blocks // 2, turn, 0, unroll=4)


def virt_kernel(places, cols_ref, vb_ref, mixed_ref, spread):
    blocks = cols_ref.shape[0]
    low = lane_ids(SUB) < BLK
    low_out = lane_ids(QJ) < BLK
    row = lax.broadcasted_iota(jnp.int32, (2 * SUB, LANES), 0)
    kept = ((row < SUB) == (lane_ids(2 * SUB) < BLK)) & ((row & (SUB - 1)) < QJ)

    def widen(k, carry):
        value = cols_ref[k].astype(jnp.float32)
        value = jnp.where(low_out, value, pltpu.roll(value, BLK, 1))
        spread[k] = jnp.concatenate([value, value], axis=0).astype(jnp.bfloat16)
        return carry

    lax.fori_loop(0, blocks, widen, 0, unroll=UNROLL)
    spread[blocks] = jnp.zeros(spread.shape[1:], spread.dtype)

    def chosen(k):
        reads = [spread[places[s, k]] for s in range(NNZ)]
        return jnp.concatenate(
            [jnp.where(low, reads[s], reads[s + 1]) for s in range(0, NNZ, 2)], axis=1
        )

    def virt(pair, carry):
        lhs = jnp.concatenate([chosen(2 * pair + n) for n in range(2)], axis=0)
        both = jnp.dot(lhs, vb_ref[pair], preferred_element_type=jnp.float32)
        mixed_ref[pair] = jnp.where(kept, both, 0.0).astype(jnp.bfloat16)
        return carry

    lax.fori_loop(0, blocks // 2, virt, 0, unroll=UNROLL)


def occ_kernel(places, mixed_ref, ob_ref, out_ref, total):
    blocks = ob_ref.shape[0]
    part = out_ref.shape[2] // BLK
    copies = out_ref.shape[0] * part // blocks
    low_out = lane_ids(QJ) < BLK
    total[...] = jnp.zeros_like(total)

    def occ(pair, carry):
        rhs = jnp.concatenate([ob_ref[2 * pair + n] for n in range(2)], axis=0)
        added = jnp.dot(mixed_ref[pair], rhs, preferred_element_type=jnp.float32)
        for n in range(2):
            for s in range(NNZ):
                place = places[NNZ + s, 2 * pair + n]
                at = (s // 2) * LANES
                total[s, place] = total[s, place] + added[n * SUB:n * SUB + QJ, at:at + LANES]
        return carry

    lax.fori_loop(0, blocks // 2, occ, 0, unroll=UNROLL)

    for a in range(0, blocks, 2):
        even = [total[0, a + n] + total[2, a + n] for n in range(2)]
        odd = [total[1, a + n] + total[3, a + n] for n in range(2)]
        moved = pltpu.roll(jnp.where(low_out, even[1], odd[0]), BLK, 1)
        value = (jnp.where(low_out, even[0], odd[1]) + moved).astype(jnp.bfloat16)
        at = a % part * BLK
        for copy in range(copies):
            out_ref[a // part * copies + copy, :, at:at + LANES] = value


def dot_kernel(part_ref, mixed_ref, early_ref, cols_ref, out_ref, raw_ref):
    part = early_ref.shape[0]
    low = lane_ids(1) < BLK
    for k in range(part):
        tail = cols_ref[part_ref[0] * part + k].astype(jnp.float32)
        last = [
            jnp.where(low, pltpu.roll(tail[2 * n:2 * n + 1], BLK, 1), tail[2 * n + 1:2 * n + 2])
            for n in range(raw_ref.shape[1] // LANES)
        ]
        last = jnp.concatenate(last, axis=1)
        block = jnp.concatenate([early_ref[k].astype(jnp.float32), last], axis=0)
        raw_ref[k * BLK:(k + 1) * BLK, :] = block.astype(jnp.bfloat16)
    summed = jnp.dot(mixed_ref[...], raw_ref[...], preferred_element_type=jnp.float32)
    out_ref[...] = summed.astype(jnp.bfloat16)


def sum_kernel(parts_ref, out_ref):
    summed = parts_ref[0].astype(jnp.float32)
    for part in range(1, parts_ref.shape[0]):
        summed = summed + parts_ref[part].astype(jnp.float32)
    out_ref[...] = summed.T


def call(kernel, outs, specs, flops, scratch=()):
    shapes = [jax.ShapeDtypeStruct(*out) for out in outs]
    single = len(shapes) == 1
    return pl.pallas_call(
        kernel,
        out_shape=shapes[0] if single else shapes,
        in_specs=specs,
        out_specs=VMEM if single else [VMEM] * len(shapes),
        scratch_shapes=list(scratch),
        compiler_params=pltpu.CompilerParams(vmem_limit_bytes=LIMIT),
        cost_estimate=pl.CostEstimate(flops=flops, bytes_accessed=1 << 20, transcendentals=0),
    )


def on_device(
    nz, ny, integrals, occ_blocks, virt_blocks, occ_partners, virt_partners, occ_counts, virt_counts
):
    blocks = NX * nz
    width = integrals.shape[1]
    rows = nz * BLK
    bf16 = jnp.bfloat16
    peers = NX * ny * NC

    packed, early = call(
        pack_kernel, [((blocks, QJ, LANES), bf16), ((BLK - 1, width), bf16)], [VMEM], 1 << 20
    )(integrals)
    columns = lax.all_to_all(packed, ("x", "z"), 0, 0, tiled=True)
    virt_near, slots = call(
        prep_kernel,
        [((blocks // 2, NNZ * BLK, 2 * BLK), bf16), ((2 * NNZ, blocks), jnp.int32)],
        [VMEM] * 5,
        1 << 28,
    )(virt_partners.T, virt_counts[None], occ_partners.T, occ_counts[None], virt_blocks)
    virt = call(
        virt_kernel,
        [((blocks // 2, 2 * SUB, LANES), bf16)],
        [SMEM, VMEM, VMEM],
        1 << 28,
        [pltpu.VMEM((blocks + 1, SUB, LANES), bf16)],
    )(slots, columns, virt_near)
    copies = call(
        occ_kernel,
        [((peers, QJ, rows), bf16)],
        [SMEM, VMEM, VMEM],
        1 << 28,
        [pltpu.VMEM((NNZ, blocks + 1, QJ, LANES), jnp.float32)],
    )(slots, virt, occ_blocks)
    copies, early = lax.optimization_barrier((copies, early))
    raw_early = lax.all_gather(early, "z", axis=0)
    mixed = lax.all_to_all(copies, ("x", "y", "c"), 0, 0, tiled=True)
    mixed, raw_early = lax.optimization_barrier((mixed, raw_early))
    partial = call(
        dot_kernel,
        [((peers * QJ, width), bf16)],
        [SMEM] + [VMEM] * 3,
        1 << 29,
        [pltpu.VMEM((rows, width), bf16)],
    )(lax.axis_index("x").reshape(1), mixed.reshape(peers * QJ, rows), raw_early, columns)
    partial = partial.reshape(NX, ny * NC * QJ, width)
    parts = lax.all_to_all(partial, "x", 0, 0, tiled=True)
    chi_tile = call(sum_kernel, [((width, ny * NC * QJ), jnp.float32)], [VMEM], 1 << 20)(parts)
    return chi_tile[:, None, :]


def solution(mesh):
    nz = mesh.shape["tens"] // NX
    ny = mesh.shape["tile"] // NC
    fine = Mesh(mesh.devices.reshape(NX, nz, ny, NC), ("x", "z", "y", "c"))
    return jax.shard_map(
        functools.partial(on_device, nz, ny),
        mesh=fine,
        in_specs=(P(("x", "z"), ("y", "c")), P(), P(), P(), P(), P(), P()),
        out_specs=P(("y", "c"), ("x", "z"), None),
        check_vma=False,
    )
```

time: 108 us -> 102 us (0.944)
  local copies, waits for them, and re-layouts: 9.61 us -> 5.13 us
  waiting for transfers between devices: 12.5 us -> 11 us
  Pallas kernels: 7.28 us -> 8.46 us
    unnamed x20 -> x14, local copies, waits for them, and re-layouts: 9.61 us -> 5.13 us
    all_to_all x1, waiting for transfers between devices: 12.5 us -> 11 us  [on_device(): columns = lax.all_to_all(packed, ('x', 'z'), 0, 0, tiled=True)]
    pallas_call x3 -> x4, Pallas kernels: 5.73 us -> 6.84 us  [the longest x1 3.41 us: on_device(): call(occ_kernel, [((peers, QJ, rows), bf16)], [SMEM, VMEM, VMEM], 1 << 28...]
where the time goes in v4:
time: 102 us
  blocking collectives  45.2 us (44%)
  starting transfers between devices  32.1 us (31%)
  waiting for transfers between devices  11 us (11%)
  Pallas kernels  8.46 us (8%)
  local copies, waits for them, and re-layouts  5.13 us (5%)
    all_gather x1, blocking collectives, on_device(): raw_early = lax.all_gather(early, 'z', axis=0)  32.9 us
    all_to_all x1, starting transfers between devices, on_device(): columns = lax.all_to_all(packed, ('x', 'z'), 0, 0, tiled=True)  22.2 us
    all_to_all x1, blocking collectives, on_device(): parts = lax.all_to_all(partial, 'x', 0, 0, tiled=True)  12.2 us
    all_to_all x1, waiting for transfers between devices, on_device(): columns = lax.all_to_all(packed, ('x', 'z'), 0, 0, tiled=True)  11 us
    all_to_all x1, starting transfers between devices, on_device(): mixed = lax.all_to_all(copies, ('x', 'y', 'c'), 0, 0, tiled=True)  9.87 us
    unnamed x14, local copies, waits for them, and re-layouts  5.13 us
    pallas_call x1, Pallas kernels, on_device(): call(occ_kernel, [((peers, QJ, rows), bf16)], [SMEM, VMEM, VMEM], 1 << 28...  3.41 us
  transfers between devices with their start and end apart: 2, of which 1 were waited for; matrix products, arithmetic and copies ran while one was open for 0% of the time, Pallas kernels for 1%

profile of v4, /device:TPU:8, one launch (start us, length us, event | category | flops | bytes accessed | tf_op | source)
XLA Modules:
  0.0 101.9 jit_solution(17951183617537633351)
XLA Ops:
  0.0 0.0 copy-start.2
  0.0 0.8 copy-done.2
  0.8 0.8 shard_map.74
  1.6 22.2 %all-to-all-start = ((bf16[64,8,128]{2,1,0:T(8,128)(2,1)}), bf16[64,8,128]{2,1,0:T(8,128)(2,1)S(1)}, u32[]{:S(2)}, u32[]{:S(2)}) async-start(bf16[64,8,128]{2,1,0:T(8,128)(2,1)} %get-tuple-element.14), calls=%async_computation | async-start | bytes 262144 | tf_op jit(solution)/shard_map/all_to_all | solution.py:170
  23.9 0.0 copy-start
  23.9 1.6 %copy-done = bf16[64,64,256]{2,1,0:T(8,128)(2,1)S(1)} copy-done((bf16[64,64,256]{2,1,0:T(8,128)(2,1)S(1)}, bf16[64,64,256]{2,1,0:T(8,128)(2,1)}, u32[]{:S(2)}) %copy-start) | copy-done | bytes 2097176
  25.5 0.0 copy-start.3
  25.5 0.7 copy-done.3
  26.1 0.0 copy-start.4
  26.1 0.7 copy-done.4
  26.8 0.0 copy-start.5
  26.8 0.7 copy-done.5
  27.5 0.0 copy-start.6
  27.5 0.7 copy-done.6
  28.1 1.1 %shard_map.73 = (bf16[32,256,128]{2,1,0:T(8,128)(2,1)S(1)}, s32[8,64]{1,0:T(8,128)S(1)}) custom-call(s32[4,64]{1,0:T(4,128)S(1)} %bitcast.14, s32[1,64]{1,0:T(1,128)S(1)} %bitcast.16, s32[4,64]{1,0:T(4,128)S(1)} %bitcast.15, s32[1,64]{1,0:T(1,128)S(1)} %bitcast.17, bf16[64,64,256]{2,1,0:T(8,128)(2,1)S(1)} %copy-done), custom_call_target="tpu_custom_call" | custom-call | flops 268435456 | bytes 1048576 | tf_op jit(solution)/shard_map/pallas_call | solution.py:171
  29.2 11.0 %all-to-all-done.cols_ref = bf16[64,8,128]{2,1,0:T(8,128)(2,1)S(1)} async-done(((bf16[64,8,128]{2,1,0:T(8,128)(2,1)}), bf16[64,8,128]{2,1,0:T(8,128)(2,1)S(1)}, u32[]{:S(2)}, u32[]{:S(2)}) %all-to-all-start) | async-done | bytes 131104 | tf_op jit(solution)/shard_map/all_to_all | solution.py:170
  40.2 0.0 copy-start.1
  40.2 1.5 %shard_map.75.mixed_ref = bf16[32,32,128]{2,1,0:T(8,128)(2,1)S(1)} custom-call(s32[8,64]{1,0:T(8,128)S(1)} %get-tuple-element.13.places, bf16[64,8,128]{2,1,0:T(8,128)(2,1)S(1)} %all-to-all-done.cols_ref, bf16[32,256,128]{2,1,0:T(8,128)(2,1)S(1)} %get-tuple-element.15.vb_ref), custom_call_target="tpu_custom_call" | custom-call | flops 268435456 | bytes 1048576 | tf_op jit(solution)/shard_map/pallas_call | solution.py:177
  41.8 0.0 copy-done.1
  41.8 3.4 %shard_map.76 = bf16[64,8,1024]{2,1,0:T(8,128)(2,1)} custom-call(s32[8,64]{1,0:T(8,128)S(1)} %get-tuple-element.13.places, bf16[32,32,128]{2,1,0:T(8,128)(2,1)S(1)} %shard_map.75.mixed_ref, bf16[64,64,256]{2,1,0:T(8,128)(2,1)S(1)} %copy-done.1), custom_call_target="tpu_custom_call" | custom-call | flops 268435456 | bytes 1048576 | tf_op jit(solution)/shard_map/pallas_call | solution.py:184
  45.2 9.9 %all-to-all-start.1 = ((bf16[64,8,1024]{2,1,0:T(8,128)(2,1)}), bf16[64,8,1024]{2,1,0:T(8,128)(2,1)S(1)}, u32[]{:S(2)}, u32[]{:S(2)}) async-start(bf16[64,8,1024]{2,1,0:T(8,128)(2,1)} %shard_map.76), calls=%async_computation.1 | async-start | bytes 2097152 | tf_op jit(solution)/shard_map/all_to_all | solution.py:193
  55.1 32.9 %all-gather.1.early_ref = bf16[16,63,512]{2,1,0:T(8,128)(2,1)S(1)} all-gather(bf16[1,63,512]{2,1,0:T(8,128)(2,1)S(1)} %bitcast.13), channel_id=2, replica_groups=mesh['x'=4,'z'=16,'y'=8,'c'=2] {'z'}, dimensions={0}, use_global_device_ids=true | all-gather | bytes 1096704 | tf_op jit(solution)/shard_map/all_gather | solution.py:192
  88.0 0.0 all-to-all-done.1
  88.0 0.8 shard_map.77
  88.8 12.2 %all_to_all.15.parts_ref = bf16[4,128,512]{2,1,0:T(8,128)(2,1)S(1)} all-to-all(bf16[4,128,512]{2,1,0:T(8,128)(2,1)S(1)} %bitcast.12), channel_id=1, replica_groups=mesh['x'=4,'z'=16,'y'=8,'c'=2] {'x'}, dimensions={0} | all-to-all | bytes 1048576 | tf_op jit(solution)/shard_map/all_to_all | solution.py:203
  101.0 0.8 shard_map.78
Async XLA Ops:
  0.0 0.8 copy-start.2
  1.6 38.6 %all-to-all-start = ((bf16[64,8,128]{2,1,0:T(8,128)(2,1)}), bf16[64,8,128]{2,1,0:T(8,128)(2,1)S(1)}, u32[]{:S(2)}, u32[]{:S(2)}) async-start(bf16[64,8,128]{2,1,0:T(8,128)(2,1)} %get-tuple-element.14), calls=%async_computation | async-start | bytes 262144 | tf_op jit(solution)/shard_map/all_to_all | solution.py:170
  23.9 1.6 %copy-start = (bf16[64,64,256]{2,1,0:T(8,128)(2,1)S(1)}, bf16[64,64,256]{2,1,0:T(8,128)(2,1)}, u32[]{:S(2)}) copy-start(bf16[64,64,256]{2,1,0:T(8,128)(2,1)} %vb_ref.1) | copy-start | bytes 6291460
  25.5 0.7 copy-start.3
  26.1 0.7 copy-start.4
  26.8 0.7 copy-start.5
  27.5 0.7 copy-start.6
  40.2 1.6 %copy-start.1 = (bf16[64,64,256]{2,1,0:T(8,128)(2,1)S(1)}, bf16[64,64,256]{2,1,0:T(8,128)(2,1)}, u32[]{:S(2)}) copy-start(bf16[64,64,256]{2,1,0:T(8,128)(2,1)} %ob_ref.1) | copy-start | bytes 6291460
  45.2 42.8 %all-to-all-start.1 = ((bf16[64,8,1024]{2,1,0:T(8,128)(2,1)}), bf16[64,8,1024]{2,1,0:T(8,128)(2,1)S(1)}, u32[]{:S(2)}, u32[]{:S(2)}) async-start(bf16[64,8,1024]{2,1,0:T(8,128)(2,1)} %shard_map.76), calls=%async_computation.1 | async-start | bytes 2097152 | tf_op jit(solution)/shard_map/all_to_all | solution.py:193

commit v5 on v4

--- a/solution.py
+++ b/solution.py
@@ -15,7 +15,7 @@
 QJ = 8
 LANES = 128
 SUB = 16
-UNROLL = 16
+UNROLL = 32
 
 VMEM = pl.BlockSpec(memory_space=pltpu.VMEM)
 SMEM = pl.BlockSpec(memory_space=pltpu.SMEM)

time: 102 us -> 102 us (level)
  no operation moved by 1% of the time
where the time goes in v5:
time: 102 us
  blocking collectives  45.2 us (44%)
  starting transfers between devices  32.1 us (31%)
  waiting for transfers between devices  11 us (11%)
  Pallas kernels  8.04 us (8%)
  local copies, waits for them, and re-layouts  5.41 us (5%)
    all_gather x1, blocking collectives, on_device(): raw_early = lax.all_gather(early, 'z', axis=0)  32.9 us
    all_to_all x1, starting transfers between devices, on_device(): columns = lax.all_to_all(packed, ('x', 'z'), 0, 0, tiled=True)  22.2 us
    all_to_all x1, blocking collectives, on_device(): parts = lax.all_to_all(partial, 'x', 0, 0, tiled=True)  12.2 us
    all_to_all x1, waiting for transfers between devices, on_device(): columns = lax.all_to_all(packed, ('x', 'z'), 0, 0, tiled=True)  11 us
    all_to_all x1, starting transfers between devices, on_device(): mixed = lax.all_to_all(copies, ('x', 'y', 'c'), 0, 0, tiled=True)  9.87 us
    unnamed x14, local copies, waits for them, and re-layouts  5.41 us
    pallas_call x1, Pallas kernels, on_device(): call(occ_kernel, [((peers, QJ, rows), bf16)], [SMEM, VMEM, VMEM], 1 << 28...  3.26 us
  transfers between devices with their start and end apart: 2, of which 1 were waited for; matrix products, arithmetic and copies ran while one was open for 0% of the time, Pallas kernels for 1%

profile of v5, /device:TPU:8, one launch (start us, length us, event | category | flops | bytes accessed | tf_op | source)
XLA Modules:
  0.0 101.7 jit_solution(6645403393538731327)
XLA Ops:
  0.0 0.0 copy-start.2
  0.0 0.8 copy-done.2
  0.8 0.8 shard_map.74
  1.6 22.2 %all-to-all-start = ((bf16[64,8,128]{2,1,0:T(8,128)(2,1)}), bf16[64,8,128]{2,1,0:T(8,128)(2,1)S(1)}, u32[]{:S(2)}, u32[]{:S(2)}) async-start(bf16[64,8,128]{2,1,0:T(8,128)(2,1)} %get-tuple-element.14), calls=%async_computation | async-start | bytes 262144 | tf_op jit(solution)/shard_map/all_to_all | solution.py:170
  23.9 0.0 copy-start
  23.9 1.6 %copy-done = bf16[64,64,256]{2,1,0:T(8,128)(2,1)S(1)} copy-done((bf16[64,64,256]{2,1,0:T(8,128)(2,1)S(1)}, bf16[64,64,256]{2,1,0:T(8,128)(2,1)}, u32[]{:S(2)}) %copy-start) | copy-done | bytes 2097176
  25.5 0.0 copy-start.3
  25.5 0.7 copy-done.3
  26.1 0.0 copy-start.4
  26.1 0.7 copy-done.4
  26.8 0.0 copy-start.5
  26.8 0.7 copy-done.5
  27.5 0.0 copy-start.6
  27.5 0.7 copy-done.6
  28.1 1.1 %shard_map.73 = (bf16[32,256,128]{2,1,0:T(8,128)(2,1)S(1)}, s32[8,64]{1,0:T(8,128)S(1)}) custom-call(s32[4,64]{1,0:T(4,128)S(1)} %bitcast.14, s32[1,64]{1,0:T(1,128)S(1)} %bitcast.16, s32[4,64]{1,0:T(4,128)S(1)} %bitcast.15, s32[1,64]{1,0:T(1,128)S(1)} %bitcast.17, bf16[64,64,256]{2,1,0:T(8,128)(2,1)S(1)} %copy-done), custom_call_target="tpu_custom_call" | custom-call | flops 268435456 | bytes 1048576 | tf_op jit(solution)/shard_map/pallas_call | solution.py:171
  29.2 11.0 %all-to-all-done.cols_ref = bf16[64,8,128]{2,1,0:T(8,128)(2,1)S(1)} async-done(((bf16[64,8,128]{2,1,0:T(8,128)(2,1)}), bf16[64,8,128]{2,1,0:T(8,128)(2,1)S(1)}, u32[]{:S(2)}, u32[]{:S(2)}) %all-to-all-start) | async-done | bytes 131104 | tf_op jit(solution)/shard_map/all_to_all | solution.py:170
  40.2 0.0 copy-start.1
  40.2 1.3 %shard_map.75.mixed_ref = bf16[32,32,128]{2,1,0:T(8,128)(2,1)S(1)} custom-call(s32[8,64]{1,0:T(8,128)S(1)} %get-tuple-element.13.places, bf16[64,8,128]{2,1,0:T(8,128)(2,1)S(1)} %all-to-all-done.cols_ref, bf16[32,256,128]{2,1,0:T(8,128)(2,1)S(1)} %get-tuple-element.15.vb_ref), custom_call_target="tpu_custom_call" | custom-call | flops 268435456 | bytes 1048576 | tf_op jit(solution)/shard_map/pallas_call | solution.py:177
  41.5 0.3 copy-done.1
  41.8 3.3 %shard_map.76 = bf16[64,8,1024]{2,1,0:T(8,128)(2,1)} custom-call(s32[8,64]{1,0:T(8,128)S(1)} %get-tuple-element.13.places, bf16[32,32,128]{2,1,0:T(8,128)(2,1)S(1)} %shard_map.75.mixed_ref, bf16[64,64,256]{2,1,0:T(8,128)(2,1)S(1)} %copy-done.1), custom_call_target="tpu_custom_call" | custom-call | flops 268435456 | bytes 1048576 | tf_op jit(solution)/shard_map/pallas_call | solution.py:184
  45.1 9.9 %all-to-all-start.1 = ((bf16[64,8,1024]{2,1,0:T(8,128)(2,1)}), bf16[64,8,1024]{2,1,0:T(8,128)(2,1)S(1)}, u32[]{:S(2)}, u32[]{:S(2)}) async-start(bf16[64,8,1024]{2,1,0:T(8,128)(2,1)} %shard_map.76), calls=%async_computation.1 | async-start | bytes 2097152 | tf_op jit(solution)/shard_map/all_to_all | solution.py:193
  54.9 32.9 %all-gather.1.early_ref = bf16[16,63,512]{2,1,0:T(8,128)(2,1)S(1)} all-gather(bf16[1,63,512]{2,1,0:T(8,128)(2,1)S(1)} %bitcast.13), channel_id=2, replica_groups=mesh['x'=4,'z'=16,'y'=8,'c'=2] {'z'}, dimensions={0}, use_global_device_ids=true | all-gather | bytes 1096704 | tf_op jit(solution)/shard_map/all_gather | solution.py:192
  87.9 0.0 all-to-all-done.1
  87.9 0.8 shard_map.77
  88.7 12.2 %all_to_all.15.parts_ref = bf16[4,128,512]{2,1,0:T(8,128)(2,1)S(1)} all-to-all(bf16[4,128,512]{2,1,0:T(8,128)(2,1)S(1)} %bitcast.12), channel_id=1, replica_groups=mesh['x'=4,'z'=16,'y'=8,'c'=2] {'x'}, dimensions={0} | all-to-all | bytes 1048576 | tf_op jit(solution)/shard_map/all_to_all | solution.py:203
  100.9 0.8 shard_map.78
Async XLA Ops:
  0.0 0.8 copy-start.2
  1.6 38.6 %all-to-all-start = ((bf16[64,8,128]{2,1,0:T(8,128)(2,1)}), bf16[64,8,128]{2,1,0:T(8,128)(2,1)S(1)}, u32[]{:S(2)}, u32[]{:S(2)}) async-start(bf16[64,8,128]{2,1,0:T(8,128)(2,1)} %get-tuple-element.14), calls=%async_computation | async-start | bytes 262144 | tf_op jit(solution)/shard_map/all_to_all | solution.py:170
  23.9 1.6 %copy-start = (bf16[64,64,256]{2,1,0:T(8,128)(2,1)S(1)}, bf16[64,64,256]{2,1,0:T(8,128)(2,1)}, u32[]{:S(2)}) copy-start(bf16[64,64,256]{2,1,0:T(8,128)(2,1)} %vb_ref.1) | copy-start | bytes 6291460
  25.5 0.7 copy-start.3
  26.1 0.7 copy-start.4
  26.8 0.7 copy-start.5
  27.5 0.7 copy-start.6
  40.2 1.6 %copy-start.1 = (bf16[64,64,256]{2,1,0:T(8,128)(2,1)S(1)}, bf16[64,64,256]{2,1,0:T(8,128)(2,1)}, u32[]{:S(2)}) copy-start(bf16[64,64,256]{2,1,0:T(8,128)(2,1)} %ob_ref.1) | copy-start | bytes 6291460
  45.1 42.8 %all-to-all-start.1 = ((bf16[64,8,1024]{2,1,0:T(8,128)(2,1)}), bf16[64,8,1024]{2,1,0:T(8,128)(2,1)S(1)}, u32[]{:S(2)}, u32[]{:S(2)}) async-start(bf16[64,8,1024]{2,1,0:T(8,128)(2,1)} %shard_map.76), calls=%async_computation.1 | async-start | bytes 2097152 | tf_op jit(solution)/shard_map/all_to_all | solution.py:193
